TPU v7x, 256 devices: a whole 4x4x8 slice. The times are simulated.
256 devices in a mesh: dp: 32 (over z, x_lo, core), fsdp: 8 (over x_hi, y).
Axes of the slice: x: 4 (x_hi: 2, x_lo: 2; x = x_hi * 2 + x_lo), y: 4, z: 8, core: 2. Of those that a mesh axis runs over, the one named last changes fastest.
Arguments:
- grads: bfloat16 [32, 2, 8192, 1024], P('dp', None, 'fsdp'), may hold values from -1.1953125 to 1.1953125
- raw_proj: float32 [2, 1024, 512], P(None, 'fsdp'), may hold values from -6 to 6
- bucket_owner: int32 [2, 512], P(None, 'fsdp'), may hold values from 0 to 31, as said below
- first_moment: float32 [2, 8, 128, 16, 512], P(None, 'fsdp', 'dp'), may hold values from -0.6 to 0.6
- second_moment: float32 [2, 8, 128, 16, 512], P(None, 'fsdp', 'dp'), may hold values from 0.01 to 0.05
Outputs:
- weight_delta: bfloat16 [2, 8192, 1024], P(None, 'fsdp')
- first_out: float32 [2, 8, 128, 16, 512], P(None, 'fsdp', 'dp')
- second_out: float32 [2, 8, 128, 16, 512], P(None, 'fsdp', 'dp')
Inputs may be any that keep to these rules, and one draw needn't show every extreme that they name: `bucket_owner`: within each matrix and each block of 64 buckets of one fsdp index, no owner holds more than 4 buckets, and one owner holds exactly 4.
All inputs are finite; a program needn't handle non-finite values.
Results may differ from a plain program's by a relative error of at most 0.0062.
Values may be sent and summed in bfloat16 or wider, within the bound.
A program may use at most 64 MiB of HBM per device.

v0:
```python
import jax
import jax.numpy as jnp
from jax import lax
from jax.sharding import PartitionSpec as P


def rows_at(table, index):
    return jax.vmap(lambda part_table, part_index: jnp.take(part_table, part_index, axis=0))(
        table, index
    )


def adam_update(first, second, grad_rows):
    new_first = 0.9 * first + 0.1 * grad_rows
    new_second = 0.999 * second + 0.001 * grad_rows * grad_rows
    scaled = (
        6.0 * (new_first / (1.0 - 0.9**10)) / (jnp.sqrt(new_second / (1.0 - 0.999**10)) + 1e-08)
    )
    return (new_first, new_second, scaled.astype(jnp.bfloat16))


def shards(grads, raw_proj, bucket_owner, first_moment, second_moment):
    matrices = grads.shape[1]
    local_rows = grads.shape[2]
    features = grads.shape[3]
    rank_width = raw_proj.shape[2]
    buckets = bucket_owner.shape[1]
    capacity = first_moment.shape[2]
    bucket_rows = local_rows // buckets
    replicas = lax.axis_size("dp")
    slot_total = replicas * capacity
    gram_part = jnp.einsum("mkr,mks->mrs", raw_proj, raw_proj, precision=lax.Precision.HIGHEST)
    gram = lax.psum(gram_part, "fsdp")
    factor = jnp.linalg.cholesky(gram)
    basis_part = lax.linalg.triangular_solve(
        factor, raw_proj, left_side=False, lower=True, transpose_a=True
    )
    basis = lax.all_gather(basis_part.astype(jnp.bfloat16), "fsdp", axis=1, tiled=True)
    projected = jnp.einsum("mdk,mkr->mdr", grads[0], basis, preferred_element_type=jnp.float32)
    blocks = projected.reshape(matrices, buckets, bucket_rows, rank_width)
    same = bucket_owner[:, :, None] == bucket_owner[:, None, :]
    earlier = jnp.arange(buckets)[None, :] < jnp.arange(buckets)[:, None]
    ranks = jnp.sum(jnp.logical_and(same, earlier).astype(jnp.int32), axis=-1)
    slots = bucket_owner * capacity + ranks
    slot_ids = jnp.arange(slot_total, dtype=jnp.int32)
    matches = slots[:, None, :] == slot_ids[None, :, None]
    occupied = jnp.any(matches, axis=2)
    bucket_of = jnp.sum(
        matches.astype(jnp.int32) * jnp.arange(buckets, dtype=jnp.int32)[None, None, :], axis=2
    )
    start = lax.axis_index("dp") * capacity
    occupied_mine = lax.dynamic_slice_in_dim(occupied, start, capacity, 1)
    totals = lax.psum(blocks, "dp")
    bucket_mine = lax.dynamic_slice_in_dim(bucket_of, start, capacity, 1)
    grad_rows = rows_at(totals, bucket_mine)
    first = first_moment[:, 0]
    second = second_moment[:, 0]
    new_first, new_second, update = adam_update(first, second, grad_rows)
    keep_mask = occupied_mine[:, :, None, None]
    first_out = jnp.where(keep_mask, new_first, first)[:, None]
    second_out = jnp.where(keep_mask, new_second, second)[:, None]
    owner_rows = jnp.einsum(
        "mcbr,mkr->mcbk", update, basis, preferred_element_type=jnp.float32
    ).astype(jnp.bfloat16)
    every_rows = lax.all_gather(owner_rows, "dp", axis=1, tiled=True)
    delta = rows_at(every_rows, slots)
    weight_delta = delta.reshape(matrices, local_rows, features)
    return (weight_delta, first_out, second_out)


def solution(mesh):
    return jax.shard_map(
        shards,
        mesh=mesh,
        in_specs=(
            P("dp", None, "fsdp", None),
            P(None, "fsdp", None),
            P(None, "fsdp"),
            P(None, "fsdp", "dp", None, None),
            P(None, "fsdp", "dp", None, None),
        ),
        out_specs=(
            P(None, "fsdp", None),
            P(None, "fsdp", "dp", None, None),
            P(None, "fsdp", "dp", None, None),
        ),
        check_vma=False,
    )
```

profile of v0, /device:TPU:1, one launch (start us, length us, event | category | flops | bytes accessed | tf_op | source)
XLA Modules:
  0.0 785.3 jit_solution(841170741054117501)
XLA Ops:
  7.2 4.3 fusion.70
  11.8 96.7 %all-reduce.4.cloned.1.call-done = f32[2,512,512]{1,2,0:T(8,128)} async-done(((f32[2,512,512]{1,2,0:T(8,128)}), f32[2,512,512]{1,2,0:T(8,128)}) %all-reduce.4.cloned.1.call-update) | async-done | bytes 2097168 | tf_op jit(solution)/shard_map/psum | solution.py:33
  108.4 3.0 copy.48
  114.9 23.5 %custom-call.34 = f32[2,128,128]{2,1,0:T(8,128)S(1)} custom-call(f32[2,128,128]{2,1,0:T(8,128)S(1)} %cholesky.274), custom_call_target="Cholesky" | custom-call | tf_op jit(solution)/shard_map/jit(cholesky)/cholesky | solution.py:34
  138.4 19.7 %custom-call.35 = f32[2,1,128,128]{2,3,1,0:T(8,128)S(1)} custom-call(f32[2,1,128,128]{3,2,1,0:T(8,128)S(1)} %select_bitcast_fusion.2), custom_call_target="InvertDiagBlocksLowerTriangular" | custom-call | tf_op jit(solution)/shard_map/jit(cholesky)/cholesky | solution.py:34
  161.4 23.5 %custom-call.36 = f32[2,128,128]{2,1,0:T(8,128)S(1)} custom-call(f32[2,128,128]{2,1,0:T(8,128)S(1)} %cholesky.278), custom_call_target="Cholesky" | custom-call | tf_op jit(solution)/shard_map/jit(cholesky)/cholesky | solution.py:34
  184.9 19.8 %custom-call.37 = f32[2,1,128,128]{2,3,1,0:T(8,128)S(1)} custom-call(f32[2,1,128,128]{3,2,1,0:T(8,128)S(1)} %get-tuple-element.32), custom_call_target="InvertDiagBlocksLowerTriangular" | custom-call | tf_op jit(solution)/shard_map/jit(cholesky)/cholesky | solution.py:34
  206.7 23.5 %custom-call.38 = f32[2,128,128]{2,1,0:T(8,128)S(1)} custom-call(f32[2,128,128]{2,1,0:T(8,128)S(1)} %cholesky.283), custom_call_target="Cholesky" | custom-call | tf_op jit(solution)/shard_map/jit(cholesky)/cholesky | solution.py:34
  230.2 19.7 %custom-call.39 = f32[2,1,128,128]{2,3,1,0:T(8,128)S(1)} custom-call(f32[2,1,128,128]{3,2,1,0:T(8,128)S(1)} %get-tuple-element.30), custom_call_target="InvertDiagBlocksLowerTriangular" | custom-call | tf_op jit(solution)/shard_map/jit(cholesky)/cholesky | solution.py:34
  251.7 23.7 %custom-call.40 = f32[2,128,128]{2,1,0:T(8,128)S(1)} custom-call(f32[2,128,128]{2,1,0:T(8,128)S(1)} %convolution_subtract_fusion.4), custom_call_target="Cholesky" | custom-call | tf_op jit(solution)/shard_map/jit(cholesky)/cholesky | solution.py:34
  277.4 14.9 %while.1 = (s32[]{:T(128)}, f32[2,512,512]{2,1,0:T(8,128)}, s32[4,2]{0,1:T(2,128)S(1)}, f32[4,2,128,128]{3,2,0,1:T(8,128)}, s32[]{:T(128)}) while((s32[]{:T(128)}, f32[2,512,512]{2,1,0:T(8,128)}, s32[4,2]{0,1:T(2,128)S(1)}, f32[4,2,128,128]{3,2,0,1:T(8,128)}, s32[]{:T(128)}) %tuple.37), condition=%wide.while_cond, body=%wide.while_body.sunk | while | flops 2 | bytes 263777 | solution.py:35
  278.1 3.1 bitcast_dynamic-update-slice_fusion.2
  281.9 3.1 bitcast_dynamic-update-slice_fusion.2
  285.6 3.1 bitcast_dynamic-update-slice_fusion.2
  289.3 3.0 bitcast_dynamic-update-slice_fusion.2
  292.3 79.4 %custom-call.41 = f32[2,4,128,128]{2,3,1,0:T(8,128)S(1)} custom-call(f32[2,4,128,128]{3,2,1,0:T(8,128)} %bitcast.129), custom_call_target="InvertDiagBlocksLowerTriangular" | custom-call | tf_op jit(solution)/shard_map/triangular_solve | solution.py:35
  378.9 62.6 %all-gather.3.cloned.1.call-done = bf16[2,1024,512]{1,2,0:T(8,128)(2,1)} async-done(((bf16[2,128,512]{1,2,0:T(8,128)(2,1)}), bf16[2,1024,512]{1,2,0:T(8,128)(2,1)}) %all-gather.3.cloned.1.call-update) | async-done | bytes 2097168 | tf_op jit(solution)/shard_map/all_gather | solution.py:38
  441.5 7.2 fusion.2
  448.7 5.4 copy.63
  455.4 235.6 %all-reduce.6.cloned.1.call-done = f32[2,64,16,512]{3,2,1,0:T(8,128)} async-done(((f32[2,64,16,512]{3,2,1,0:T(8,128)}), f32[2,64,16,512]{3,2,1,0:T(8,128)}) %all-reduce.6.cloned.1.call-update) | async-done | bytes 4194320 | tf_op jit(solution)/shard_map/psum | solution.py:53
  691.0 2.8 gather_fusion
  696.7 71.6 %all-gather.5.cloned.1.call-done = bf16[2,128,16,1024]{3,2,1,0:T(8,128)(2,1)} async-done(((bf16[2,4,16,1024]{3,2,1,0:T(8,128)(2,1)}), bf16[2,128,16,1024]{3,2,1,0:T(8,128)(2,1)}) %all-gather.5.cloned.1.call-update) | async-done | bytes 8388624 | tf_op jit(solution)/shard_map/all_gather | solution.py:65
  768.3 6.3 gather_fusion.1
  774.5 3.9 bitcast_select_fusion
  (78 shorter events, 26.6 us)
Async XLA Ops:
  7.2 101.3 %all-reduce.4.cloned.1.call-start = ((), (), s32[]{:S(2)}) async-start(), calls=%async_computation | async-start | bytes 4194304 | tf_op jit(solution)/shard_map/psum | solution.py:33
  11.6 429.9 %all-gather.3.cloned.1.call-start = ((), (), s32[]{:S(2)}) async-start(), calls=%async_computation.1 | async-start | bytes 2359296 | tf_op jit(solution)/shard_map/all_gather | solution.py:38
  108.4 3.0 copy-start
  113.6 1.3 copy-start.1
  275.7 96.1 %copy-start.2 = (f32[2,128,512]{2,1,0:T(8,128)S(1)}, f32[2,128,512]{2,1,0:T(8,128)}, u32[]{:S(2)}) copy-start(f32[2,128,512]{2,1,0:T(8,128)} %param.6) | copy-start | bytes 1572868
  378.9 312.2 %all-reduce.6.cloned.1.call-start = ((), (), s32[]{:S(2)}) async-start(), calls=%async_computation.2 | async-start | bytes 8388608 | tf_op jit(solution)/shard_map/psum | solution.py:53
  454.1 0.7 copy-start.6
  454.1 239.6 %copy-start.3 = (bf16[2,1024,512]{1,2,0:T(8,128)(2,1)S(1)}, bf16[2,1024,512]{1,2,0:T(8,128)(2,1)}, u32[]{:S(2)}) copy-start(bf16[2,1024,512]{1,2,0:T(8,128)(2,1)} %all-gather.3.cloned.1.call-done) | copy-start | bytes 6291460
  454.2 239.6 %copy-start.4 = (f32[2,1,4,16,512]{4,3,2,1,0:T(8,128)S(1)}, f32[2,1,4,16,512]{4,3,2,1,0:T(8,128)}, u32[]{:S(2)}) copy-start(f32[2,1,4,16,512]{4,3,2,1,0:T(8,128)} %param.9) | copy-start | bytes 786436
  454.2 239.6 %copy-start.5 = (f32[2,1,4,16,512]{4,3,2,1,0:T(8,128)S(1)}, f32[2,1,4,16,512]{4,3,2,1,0:T(8,128)}, u32[]{:S(2)}) copy-start(f32[2,1,4,16,512]{4,3,2,1,0:T(8,128)} %param.8) | copy-start | bytes 786436
  454.2 314.1 %all-gather.5.cloned.1.call-start = ((), (), s32[]{:S(2)}) async-start(), calls=%async_computation.3 | async-start | bytes 8650752 | tf_op jit(solution)/shard_map/all_gather | solution.py:65
Sparse Core Ops, SparseCore 0:
  11.7 96.6 all-reduce.3
  379.0 62.5 all-gather.2
  454.3 236.6 all-reduce.5
  695.3 72.9 all-gather.4
where the time goes:
time: 796 us; the launch traced here: 785 us
  waiting for transfers between devices  467 us (59%)
  other arithmetic  243 us (31%)
  local copies, waits for them, and re-layouts  35 us (4%)
  matrix products  26 us (3%)
  between operations  14.5 us (2%)
    psum x1, waiting for transfers between devices, shards(): totals = lax.psum(blocks, 'dp')  236 us
    another operation x16, other arithmetic, shards(): factor = jnp.linalg.cholesky(gram)  154 us
    psum x1, waiting for transfers between devices, shards(): gram = lax.psum(gram_part, 'fsdp')  96.7 us
    another operation x5, other arithmetic, shards(): lax.linalg.triangular_solve(factor, raw_proj, left_side=False, lower=True...  82 us
    all_gather x1, waiting for transfers between devices, shards(): every_rows = lax.all_gather(owner_rows, 'dp', axis=1, tiled=True)  71.6 us
    all_gather x1, waiting for transfers between devices, shards(): lax.all_gather(basis_part.astype(jnp.bfloat16), 'fsdp', axis=1, tiled=True)  62.6 us
  transfers between devices with their start and end apart: 4, of which 4 were waited for; matrix products, arithmetic and copies ran while one was open for 0% of the time, Pallas kernels for 0%

commit v1 on v0

--- a/solution.py
+++ b/solution.py
@@ -62,7 +62,9 @@
     owner_rows = jnp.einsum(
         "mcbr,mkr->mcbk", update, basis, preferred_element_type=jnp.float32
     ).astype(jnp.bfloat16)
-    every_rows = lax.all_gather(owner_rows, "dp", axis=1, tiled=True)
+    every_rows = jnp.concatenate(
+        lax.all_to_all(jnp.stack([owner_rows] * lax.axis_size("dp")), "dp", 0, 0), axis=1
+    )
     delta = rows_at(every_rows, slots)
     weight_delta = delta.reshape(matrices, local_rows, features)
     return (weight_delta, first_out, second_out)

time: 796 us -> 929 us (1.17)
  waiting for transfers between devices: 467 us -> 580 us
  local copies, waits for them, and re-layouts: 35 us -> 48 us
    all_to_all x0 -> x1, waiting for transfers between devices: none -> 185 us  [shards(): lax.all_to_all(jnp.stack([owner_rows] * lax.axis_size('dp')), 'dp', 0, 0)]
    all_gather x1 -> x0, waiting for transfers between devices: 71.6 us -> none  [shards(): every_rows = lax.all_gather(owner_rows, 'dp', axis=1, tiled=True)]
    another operation x12 -> x13, local copies, waits for them, and re-layouts: 14.9 us -> 19.2 us
where the time goes in v1:
time: 929 us; the launch traced here: 918 us
  waiting for transfers between devices  580 us (62%)
  other arithmetic  243 us (26%)
  local copies, waits for them, and re-layouts  48 us (5%)
  matrix products  25.3 us (3%)
  between operations  14.3 us (2%)
    psum x1, waiting for transfers between devices, shards(): totals = lax.psum(blocks, 'dp')  236 us
    all_to_all x1, waiting for transfers between devices, shards(): lax.all_to_all(jnp.stack([owner_rows] * lax.axis_size('dp')), 'dp', 0, 0)  185 us
    another operation x16, other arithmetic, shards(): factor = jnp.linalg.cholesky(gram)  154 us
    psum x1, waiting for transfers between devices, shards(): gram = lax.psum(gram_part, 'fsdp')  96.6 us
    another operation x5, other arithmetic, shards(): lax.linalg.triangular_solve(factor, raw_proj, left_side=False, lower=True...  82 us
    all_gather x1, waiting for transfers between devices, shards(): lax.all_gather(basis_part.astype(jnp.bfloat16), 'fsdp', axis=1, tiled=True)  62.6 us
  transfers between devices with their start and end apart: 4, of which 4 were waited for; matrix products, arithmetic and copies ran while one was open for 0% of the time, Pallas kernels for 0%

profile of v1, /device:TPU:1, one launch (start us, length us, event | category | flops | bytes accessed | tf_op | source)
XLA Modules:
  0.0 918.3 jit_solution(2003758061917355047)
XLA Ops:
  7.2 4.4 fusion.70
  11.8 96.6 %all-reduce.4.cloned.1.call-done = f32[2,512,512]{1,2,0:T(8,128)} async-done(((f32[2,512,512]{1,2,0:T(8,128)}), f32[2,512,512]{1,2,0:T(8,128)}) %all-reduce.4.cloned.1.call-update) | async-done | bytes 2097168 | tf_op jit(solution)/shard_map/psum | solution.py:33
  114.9 23.5 %custom-call.34 = f32[2,128,128]{2,1,0:T(8,128)S(1)} custom-call(f32[2,128,128]{2,1,0:T(8,128)S(1)} %cholesky.274), custom_call_target="Cholesky" | custom-call | tf_op jit(solution)/shard_map/jit(cholesky)/cholesky | solution.py:34
  138.4 19.7 %custom-call.35 = f32[2,1,128,128]{2,3,1,0:T(8,128)S(1)} custom-call(f32[2,1,128,128]{3,2,1,0:T(8,128)S(1)} %select_bitcast_fusion.2), custom_call_target="InvertDiagBlocksLowerTriangular" | custom-call | tf_op jit(solution)/shard_map/jit(cholesky)/cholesky | solution.py:34
  161.3 23.5 %custom-call.36 = f32[2,128,128]{2,1,0:T(8,128)S(1)} custom-call(f32[2,128,128]{2,1,0:T(8,128)S(1)} %cholesky.278), custom_call_target="Cholesky" | custom-call | tf_op jit(solution)/shard_map/jit(cholesky)/cholesky | solution.py:34
  184.8 20.1 %custom-call.37 = f32[2,1,128,128]{2,3,1,0:T(8,128)S(1)} custom-call(f32[2,1,128,128]{3,2,1,0:T(8,128)S(1)} %get-tuple-element.32), custom_call_target="InvertDiagBlocksLowerTriangular" | custom-call | tf_op jit(solution)/shard_map/jit(cholesky)/cholesky | solution.py:34
  206.9 23.5 %custom-call.38 = f32[2,128,128]{2,1,0:T(8,128)S(1)} custom-call(f32[2,128,128]{2,1,0:T(8,128)S(1)} %cholesky.283), custom_call_target="Cholesky" | custom-call | tf_op jit(solution)/shard_map/jit(cholesky)/cholesky | solution.py:34
  230.4 19.7 %custom-call.39 = f32[2,1,128,128]{2,3,1,0:T(8,128)S(1)} custom-call(f32[2,1,128,128]{3,2,1,0:T(8,128)S(1)} %get-tuple-element.30), custom_call_target="InvertDiagBlocksLowerTriangular" | custom-call | tf_op jit(solution)/shard_map/jit(cholesky)/cholesky | solution.py:34
  251.9 23.6 %custom-call.40 = f32[2,128,128]{2,1,0:T(8,128)S(1)} custom-call(f32[2,128,128]{2,1,0:T(8,128)S(1)} %convolution_subtract_fusion.4), custom_call_target="Cholesky" | custom-call | tf_op jit(solution)/shard_map/jit(cholesky)/cholesky | solution.py:34
  277.7 14.9 %while.1 = (s32[]{:T(128)}, f32[2,512,512]{2,1,0:T(8,128)}, s32[4,2]{0,1:T(2,128)S(1)}, f32[4,2,128,128]{3,2,0,1:T(8,128)}, s32[]{:T(128)}) while((s32[]{:T(128)}, f32[2,512,512]{2,1,0:T(8,128)}, s32[4,2]{0,1:T(2,128)S(1)}, f32[4,2,128,128]{3,2,0,1:T(8,128)}, s32[]{:T(128)}) %tuple.37), condition=%wide.while_cond, body=%wide.while_body.sunk | while | flops 2 | bytes 263777 | solution.py:35
  278.3 3.1 bitcast_dynamic-update-slice_fusion.2
  282.1 3.1 bitcast_dynamic-update-slice_fusion.2
  285.8 3.1 bitcast_dynamic-update-slice_fusion.2
  292.6 79.4 %custom-call.41 = f32[2,4,128,128]{2,3,1,0:T(8,128)S(1)} custom-call(f32[2,4,128,128]{3,2,1,0:T(8,128)} %bitcast.133), custom_call_target="InvertDiagBlocksLowerTriangular" | custom-call | tf_op jit(solution)/shard_map/triangular_solve | solution.py:35
  379.1 62.6 %all-gather.2.cloned.1.call-done = bf16[2,1024,512]{1,2,0:T(8,128)(2,1)} async-done(((bf16[2,128,512]{1,2,0:T(8,128)(2,1)}), bf16[2,1024,512]{1,2,0:T(8,128)(2,1)}) %all-gather.2.cloned.1.call-update) | async-done | bytes 2097168 | tf_op jit(solution)/shard_map/all_gather | solution.py:38
  441.8 7.2 fusion.2
  449.0 5.6 copy.86
  455.8 235.7 %all-reduce.6.cloned.1.call-done = f32[2,64,16,512]{3,2,1,0:T(8,128)} async-done(((f32[2,64,16,512]{3,2,1,0:T(8,128)}), f32[2,64,16,512]{3,2,1,0:T(8,128)}) %all-reduce.6.cloned.1.call-update) | async-done | bytes 4194320 | tf_op jit(solution)/shard_map/psum | solution.py:53
  694.9 4.3 stack.2
  699.2 7.1 all-to-all-start
  707.8 185.1 %all-to-all-done = bf16[32,2,4,16,1024]{4,3,2,1,0:T(8,128)(2,1)} async-done(((bf16[32,2,4,16,1024]{4,3,2,1,0:T(8,128)(2,1)}), bf16[32,2,4,16,1024]{4,3,2,1,0:T(8,128)(2,1)}, u32[]{:S(2)}, u32[]{:S(2)}) %all-to-all-start) | async-done | bytes 8388640 | tf_op jit(solution)/shard_map/all_to_all | solution.py:66
  892.9 8.5 copy.89
  901.4 6.3 gather_fusion.1
  907.7 3.9 bitcast_select_fusion
  (79 shorter events, 34.7 us)
Async XLA Ops:
  7.2 101.3 %all-reduce.4.cloned.1.call-start = ((), (), s32[]{:S(2)}) async-start(), calls=%async_computation.1 | async-start | bytes 4194304 | tf_op jit(solution)/shard_map/psum | solution.py:33
  11.6 430.2 %all-gather.2.cloned.1.call-start = ((), (), s32[]{:S(2)}) async-start(), calls=%async_computation.2 | async-start | bytes 2359296 | tf_op jit(solution)/shard_map/all_gather | solution.py:38
  108.4 3.0 copy-start
  113.5 1.3 copy-start.1
  275.9 96.1 %copy-start.2 = (f32[2,128,512]{2,1,0:T(8,128)S(1)}, f32[2,128,512]{2,1,0:T(8,128)}, u32[]{:S(2)}) copy-start(f32[2,128,512]{2,1,0:T(8,128)} %param.6) | copy-start | bytes 1572868
  379.1 312.4 %all-reduce.6.cloned.1.call-start = ((), (), s32[]{:S(2)}) async-start(), calls=%async_computation.3 | async-start | bytes 8388608 | tf_op jit(solution)/shard_map/psum | solution.py:53
  454.6 0.7 copy-start.6
  454.6 239.7 %copy-start.3 = (bf16[2,1024,512]{1,2,0:T(8,128)(2,1)S(1)}, bf16[2,1024,512]{1,2,0:T(8,128)(2,1)}, u32[]{:S(2)}) copy-start(bf16[2,1024,512]{1,2,0:T(8,128)(2,1)} %all-gather.2.cloned.1.call-done) | copy-start | bytes 6291460
  454.6 239.7 %copy-start.4 = (f32[2,1,4,16,512]{4,3,2,1,0:T(8,128)S(1)}, f32[2,1,4,16,512]{4,3,2,1,0:T(8,128)}, u32[]{:S(2)}) copy-start(f32[2,1,4,16,512]{4,3,2,1,0:T(8,128)} %param.9) | copy-start | bytes 786436
  454.6 239.7 %copy-start.5 = (f32[2,1,4,16,512]{4,3,2,1,0:T(8,128)S(1)}, f32[2,1,4,16,512]{4,3,2,1,0:T(8,128)}, u32[]{:S(2)}) copy-start(f32[2,1,4,16,512]{4,3,2,1,0:T(8,128)} %param.8) | copy-start | bytes 786436
  699.2 193.7 %all-to-all-start = ((bf16[32,2,4,16,1024]{4,3,2,1,0:T(8,128)(2,1)}), bf16[32,2,4,16,1024]{4,3,2,1,0:T(8,128)(2,1)}, u32[]{:S(2)}, u32[]{:S(2)}) async-start(bf16[32,2,4,16,1024]{4,3,2,1,0:T(8,128)(2,1)} %stack.2), calls=%async_computation | async-start | bytes 16777216 | tf_op jit(solution)/shard_map/all_to_all | solution.py:66
Sparse Core Ops, SparseCore 0:
  11.7 96.6 all-reduce.3
  379.2 62.5 all-gather.1
  454.7 236.6 all-reduce.5
